TPU v7x, 32 devices: a whole 2x2x4 slice. The times are simulated.
32 devices in a mesh: groups: 2 (over y), tp: 16 (over z, x, core).
Axes of the slice: x: 2, y: 2, z: 4, core: 2. Of those that a mesh axis runs over, the one named last changes fastest.
Arguments:
- hidden_in: bfloat16 [32, 8, 512], P(('groups', 'tp')), parts along dimension 0, may hold values from -6 to 6
- norm_gain: float32 [8192], replicated, may hold values from 0.1 to 1.9
- q_blocks: bfloat16 [16, 16, 128, 2048], P('tp'), may hold values from -0.0625 to 0.0625
- o_blocks: bfloat16 [16, 2048, 16, 128], P('tp'), may hold values from -1.5 to 1.5
- kv_blocks: bfloat16 [2, 1024, 8192], P(None, None, 'tp'), may hold values from -0.0625 to 0.0625
- kv_assign: int32 [16], replicated, may hold values from 0 to 7, as said below
- key_cache: bfloat16 [32, 8, 2048, 128], P(('groups', 'tp')), parts along dimension 0, may hold values from -240 to 240
- value_cache: bfloat16 [32, 8, 2048, 128], P(('groups', 'tp')), parts along dimension 0, may hold values from -6 to 6
- lengths: int32 [32, 8], P(('groups', 'tp')), parts along dimension 0, may hold values from 1 to 2048, as said below
Outputs:
- attn_out: bfloat16 [32, 8, 512], P(('groups', 'tp')), parts along dimension 0
There are 2 independent parts, one for each index of `groups`. A program takes and returns all parts, laid end to end along the dimension named above; an argument that names none is the same for every part. Nothing has to cross between parts.
Inputs may be any that keep to these rules, and one draw needn't show every extreme that they name: `kv_assign`: entries 2m and 2m + 1 are equal, and each of the 8 key-value heads is named by exactly two entries. `lengths`: in every rank one row has all 2048 positions valid.
All inputs are finite; a program needn't handle non-finite values.
Results may differ from a plain program's by a relative error of at most 0.011.
The roundings to bfloat16 on the way count: a program that leaves them out, or rounds other values in their place, can miss the bound.
Values may be sent and summed in bfloat16 or wider, within the bound.
A program may use at most 128 MiB of HBM per device.

v0:
```python
import jax
import jax.numpy as jnp
from jax import lax
from jax.sharding import PartitionSpec as P

D = 8192
KVH = 8
HD = 128
ROLL = 16
ROWS = 8
GR = 4
QG = 16
DS = 512


def from_partner(value, axis, bit):
    mask = 2**bit
    pairs = [(source, source ^ mask) for source in range(lax.axis_size(axis))]
    return lax.ppermute(value, axis, pairs)


def norm_rows(rows_float, norm_gain):
    mean_square = jnp.mean(rows_float * rows_float, axis=-1, keepdims=True)
    return (rows_float * lax.rsqrt(mean_square + 1e-05) * norm_gain[None, :]).astype(jnp.bfloat16)


def local(
    hidden_in, norm_gain, q_blocks, o_blocks, kv_blocks, kv_assign, key_cache, value_cache, lengths
):
    ranks = lax.axis_size("tp")
    my_index = lax.axis_index("tp")
    my_rank = my_index % ROLL
    my_half = my_rank % 2
    grid_cols = ranks // GR
    group_count = ranks // ROLL
    col_width = q_blocks.shape[3]
    key_width = kv_blocks.shape[2]
    grid_row = my_index // grid_cols
    grid_col = my_index % grid_cols
    dest_ids = jnp.arange(ranks, dtype=jnp.int32)
    dest_rank = dest_ids % ROLL
    dest_head = kv_assign[dest_rank]
    dest_group = 2 * dest_head + dest_rank % 2
    dest_copy = dest_ids // ROLL
    every_rows = lax.all_gather(hidden_in, "tp", axis=0, tiled=True)
    rows_float = (
        every_rows.reshape(group_count, ROLL, ROWS, DS)
        .transpose(0, 2, 1, 3)
        .reshape(group_count * ROWS, D)
        .astype(jnp.float32)
    )
    normed_every = norm_rows(rows_float, norm_gain)
    col_rows = lax.dynamic_slice_in_dim(normed_every, grid_col * col_width, col_width, 1)
    query_part = jnp.einsum(
        "rc,aec->rae", col_rows, q_blocks[0], preferred_element_type=jnp.float32
    )
    query_part = (
        query_part.reshape(group_count, ROWS, QG, HD)
        .transpose(0, 2, 1, 3)
        .reshape(group_count * QG, ROWS, HD)
    )
    query_pick = jnp.take(query_part, dest_copy * QG + dest_group, axis=0)
    slot_mask = (jnp.arange(GR, dtype=jnp.int32) == grid_row).astype(jnp.float32)
    query_term = (query_pick[:, :, None, :] * slot_mask[None, None, :, None]).reshape(
        ranks, ROWS, GR * HD
    )
    key_rows = lax.dynamic_slice_in_dim(normed_every, my_index * key_width, key_width, 1)
    keyval_part = jnp.einsum("rc,kfc->rkf", key_rows, kv_blocks, preferred_element_type=jnp.float32)
    keyval_part = (
        keyval_part.reshape(group_count, ROWS, 2, KVH, HD)
        .transpose(0, 3, 1, 2, 4)
        .reshape(group_count * KVH, ROWS, 2 * HD)
    )
    keyval_term = jnp.take(keyval_part, dest_copy * KVH + dest_head, axis=0)
    proj_term = jnp.concatenate([query_term, keyval_term], -1).reshape(ranks * ROWS, (GR + 2) * HD)
    projected = lax.psum_scatter(proj_term, "tp", scatter_dimension=0, tiled=True)
    queries = projected[:, : GR * HD].astype(jnp.bfloat16)
    keyval_new = projected[:, GR * HD :].astype(jnp.bfloat16)
    key_new = keyval_new[:, :HD]
    value_new = keyval_new[:, HD:]
    partner_queries = from_partner(queries, "tp", 0)
    both_queries = jnp.where(
        my_half == 0,
        jnp.concatenate([queries, partner_queries], 1),
        jnp.concatenate([partner_queries, queries], 1),
    )
    both_queries = both_queries.reshape(ROWS, 2 * GR, HD)
    scale = 1.0 / HD**0.5
    scores = (
        jnp.einsum("bhe,bte->bht", both_queries, key_cache[0], preferred_element_type=jnp.float32)
        * scale
    )
    positions = jnp.arange(scores.shape[2], dtype=jnp.int32)
    masked = positions[None, None, :] < lengths[0][:, None, None]
    new_score = (
        jnp.einsum("bhe,be->bh", both_queries, key_new, preferred_element_type=jnp.float32) * scale
    )
    new_score = jnp.where(my_half == 0, new_score, jnp.float32(-1e30))
    top = jnp.maximum(jnp.max(jnp.where(masked, scores, jnp.float32(-1e30)), axis=-1), new_score)
    weights = jnp.where(masked, jnp.exp(scores - top[..., None]), jnp.float32(0.0))
    new_weight = jnp.exp(new_score - top)
    total = jnp.sum(weights, axis=-1) + new_weight
    summed = jnp.einsum(
        "bht,bte->bhe",
        weights.astype(jnp.bfloat16),
        value_cache[0],
        preferred_element_type=jnp.float32,
    )
    new_rounded = lax.optimization_barrier(new_weight.astype(jnp.bfloat16)).astype(jnp.float32)
    summed = summed + new_rounded[..., None] * value_new.astype(jnp.float32)[:, None, :]
    top_split = top.reshape(ROWS, 2, GR)
    total_split = total.reshape(ROWS, 2, GR)
    summed_split = summed.reshape(ROWS, 2, GR, HD)
    first_half = my_half == 0
    own_top = jnp.where(first_half, top_split[:, 0], top_split[:, 1])
    own_total = jnp.where(first_half, total_split[:, 0], total_split[:, 1])
    own_summed = jnp.where(first_half, summed_split[:, 0], summed_split[:, 1])
    give_top = jnp.where(first_half, top_split[:, 1], top_split[:, 0])
    give_total = jnp.where(first_half, total_split[:, 1], total_split[:, 0])
    give_summed = jnp.where(first_half, summed_split[:, 1], summed_split[:, 0])
    got_top, got_total, got_summed = from_partner((give_top, give_total, give_summed), "tp", 0)
    joint = jnp.maximum(own_top, got_top)
    factor_own = jnp.exp(own_top - joint)
    factor_got = jnp.exp(got_top - joint)
    numer = own_summed * factor_own[..., None] + got_summed * factor_got[..., None]
    denom = own_total * factor_own + got_total * factor_got
    attention = (numer / denom[..., None]).astype(jnp.bfloat16).reshape(ROWS, GR * HD)
    every_attn = lax.all_gather(attention[None], "tp", axis=0, tiled=True)
    head_ids = jnp.arange(KVH, dtype=jnp.int32)
    pair_heads = kv_assign[0::2]
    inverse = jnp.sum(
        head_ids[None, :] * (pair_heads[None, :] == head_ids[:, None]).astype(jnp.int32), axis=1
    )
    slot_ids = jnp.arange(QG, dtype=jnp.int32)
    rank_of_slot = 2 * inverse[slot_ids // 2] + slot_ids % 2
    attn_grid = every_attn.reshape(group_count, ROLL, ROWS, GR, HD)
    row_slot = lax.dynamic_index_in_dim(attn_grid, grid_row, 3, keepdims=False)
    chosen = jnp.take(row_slot, rank_of_slot, axis=1)
    out_part = jnp.einsum("gabe,cae->gbc", chosen, o_blocks[0], preferred_element_type=jnp.float32)
    placed = jnp.zeros((group_count, ROWS, D), jnp.float32)
    placed = lax.dynamic_update_slice_in_dim(placed, out_part, grid_col * col_width, 2)
    out_term = (
        placed.reshape(group_count, ROWS, ROLL, DS).transpose(0, 2, 1, 3).reshape(ranks * ROWS, DS)
    )
    my_cols = lax.psum_scatter(out_term, "tp", scatter_dimension=0, tiled=True)
    return my_cols.astype(jnp.bfloat16)[None]


def solution(mesh):
    return jax.shard_map(
        local,
        mesh=mesh,
        in_specs=(
            P(("groups", "tp"), None, None),
            P(),
            P("tp", None, None, None),
            P("tp", None, None, None),
            P(None, None, "tp"),
            P(),
            P(("groups", "tp"), None, None, None),
            P(("groups", "tp"), None, None, None),
            P(("groups", "tp"), None),
        ),
        out_specs=P(("groups", "tp"), None, None),
        check_vma=False,
    )
```

profile of v0, /device:TPU:0, one launch (start us, length us, event | category | flops | bytes accessed | tf_op | source)
XLA Modules:
  0.0 194.6 jit_solution(7086260716293882496)
XLA Ops:
  6.5 23.8 %all_gather.6 = bf16[16,8,512]{2,1,0:T(8,128)(2,1)S(1)} all-gather(bf16[1,8,512]{2,1,0:T(8,128)(2,1)} %param.9), channel_id=1, replica_groups=mesh['groups'=2,'tp'=16] {'tp'}, dimensions={0}, use_global_device_ids=true | all-gather | bytes 139264 | tf_op jit(solution)/shard_map/all_gather | solution.py:45
  30.3 0.2 multiply_reduce_fusion
  30.6 0.7 slice.41
  31.3 1.3 gather_fusion.1
  32.7 0.1 select_reduce_fusion.1
  32.8 0.7 gather_fusion
  33.5 0.1 broadcast_bitcast_fusion
  33.6 0.9 multiply_convert_fusion
  34.4 0.6 convolution_bitcast_fusion
  35.1 0.1 broadcast_in_dim.83
  35.2 0.1 broadcast_in_dim.84
  35.3 0.0 copy-start.2
  35.3 5.6 %fusion.17 = f32[16,8,128]{2,1,0:T(8,128)S(1)} fusion(bf16[1,16,128,2048]{3,2,1,0:T(8,128)(2,1)} %param.11, bf16[8,8192]{1,0:T(8,128)(2,1)S(1)} %multiply_convert_fusion, s32[]{:T(128)S(6)} %select_n.308), kind=kOutput, calls=%fused_computation.16 | convolution fusion | flops 67108864 | bytes 8486916 | tf_op jit(solution)/shard_map/rc,aec->rae/dot_general | solution.py:54
  41.0 0.6 gather_fusion.2
  41.5 0.1 broadcast_select_fusion
  41.7 0.6 gather_fusion.3
  42.2 0.1 bitcast_select_fusion
  42.3 0.8 pad_maximum_fusion
  43.1 0.0 reduce-scatter.3.cloned.1.call-update
  43.1 0.0 reduce-scatter.5.cloned.1.call-start
  43.3 0.1 iota_compare_fusion
  43.3 52.8 %reduce-scatter.3.cloned.1.call-done = f32[8,768]{1,0:T(8,128)} async-done(((f32[128,768]{1,0:T(8,128)}), f32[8,768]{1,0:T(8,128)}) %reduce-scatter.3.cloned.1.call-update) | async-done | bytes 24592 | tf_op jit(solution)/shard_map/reduce_scatter | solution.py:76
  96.1 0.7 convert.7
  96.9 0.0 collective-permute-start
  96.9 1.2 collective-permute-done
  98.1 0.1 fusion.41
  98.2 3.5 %select_reduce_fusion = (f32[8,8]{1,0:T(8,128)S(1)}, f32[8,8,2048]{2,1,0:T(8,128)S(1)}) fusion(pred[8,2048]{1,0:T(8,128)(4,1)S(1)} %iota_compare_fusion, bf16[1,8,2048,128]{3,2,1,0:T(8,128)(2,1)} %param.15, bf16[8,4,128]{2,1,0:T(4,128)(2,1)S(1)} %concatenate.18, bf16[8,4,128]{2,1,0:T(4,128)(2,1)S(1)} %concatenate.17, pred[]{:T(512)S(6)} %eq.39), kind=kOutput, calls=%fused_computation.20 | convolution fusion | flops 34021312 | bytes 4751617 | tf_op jit(solution)/shard_map/bhe,bte->bht/dot_general | solution.py:90
  101.7 0.1 copy.45
  101.8 0.2 collective-permute-start.1
  101.9 0.3 fusion.23
  102.2 0.1 copy.50
  102.3 0.3 collective-permute-start.3
  102.6 2.9 %fusion.20 = f32[8,8,128]{2,1,0:T(8,128)S(1)} fusion(bf16[1,8,2048,128]{3,2,1,0:T(8,128)(2,1)} %param.16, f32[8,8,2048]{2,1,0:T(8,128)S(1)} %get-tuple-element.17, f32[8,8]{1,0:T(8,128)S(1)} %fusion.43, pred[8,2048]{1,0:T(8,128)(4,1)S(1)} %iota_compare_fusion, f32[8,128]{1,0:T(8,128)S(1)} %get-tuple-element.8, f32[8,8]{1,0:T(8,128)S(1)} %convert_element_type.57), kind=kOutput, calls=%fused_computation.18 | convolution fusion | flops 33964032 | bytes 4772352 | tf_op jit(solution)/shard_map/bht,bte->bhe/dot_general | solution.py:103
  105.6 0.2 collective-permute-start.2
  105.8 0.0 collective-permute-done.1
  105.8 0.0 collective-permute-done.3
  105.8 0.1 copy.46
  105.9 0.1 copy.49
  106.0 0.1 copy.51
  106.1 0.8 collective-permute-done.2
  106.8 0.1 fusion.38
  106.9 19.8 %all_gather.7 = bf16[16,8,512]{2,1,0:T(8,128)(2,1)S(1)} all-gather(bf16[1,8,512]{2,1,0:T(8,128)(2,1)S(1)} %broadcast_in_dim_reshape.3), channel_id=1, replica_groups=mesh['groups'=2,'tp'=16] {'tp'}, dimensions={0}, use_global_device_ids=true | all-gather | bytes 139264 | tf_op jit(solution)/shard_map/all_gather | solution.py:128
  126.7 0.6 gather_fusion.4
  127.3 5.7 %fusion.14 = f32[1,8,8192]{2,1,0:T(8,128)S(1)} fusion(f32[1,8,8192]{2,1,0:T(8,128)S(1)} %broadcast_in_dim.78, s32[]{:T(128)S(6)} %select_n.308, bf16[2048,16,128]{2,1,0:T(8,128)(2,1)} %bitcast.146, bf16[16,8,128]{2,1,0:T(8,128)(2,1)S(1)} %gather_fusion.4, pred[16]{0:T(512)(128)(4,1)S(1)} %get-tuple-element.18), kind=kOutput, calls=%fused_computation.15 | convolution fusion | flops 67125248 | bytes 8487428 | tf_op jit(solution)/shard_map/gabe,cae->gbc/dot_general | solution.py:139
  132.9 0.7 copy-done.1
  133.6 0.0 reduce-scatter.5.cloned.1.call-update
  133.7 52.8 %reduce-scatter.5.cloned.1.call-done = f32[8,512]{1,0:T(8,128)} async-done(((f32[128,512]{1,0:T(8,128)}), f32[8,512]{1,0:T(8,128)}) %reduce-scatter.5.cloned.1.call-update) | async-done | bytes 16400 | tf_op jit(solution)/shard_map/reduce_scatter | solution.py:145
  186.4 1.3 convert_bitcast_fusion
  (33 shorter events, 0.3 us)
Async XLA Ops:
  6.5 27.9 %copy-start = (bf16[2,1024,512]{2,1,0:T(8,128)(2,1)S(1)}, bf16[2,1024,512]{2,1,0:T(8,128)(2,1)}, u32[]{:S(2)}) copy-start(bf16[2,1024,512]{2,1,0:T(8,128)(2,1)} %param.13) | copy-start | bytes 6291460
  6.5 89.6 %reduce-scatter.3.cloned.1.call-start = ((), (), s32[]{:S(2)}) async-start(), calls=%async_computation.2 | async-start | bytes 417792 | tf_op jit(solution)/shard_map/reduce_scatter | solution.py:76
  35.3 8.0 %copy-start.2 = (s32[1,8]{1,0:T(1,128)S(1)}, s32[1,8]{1,0:T(1,128)}, u32[]{:S(2)}) copy-start(s32[1,8]{1,0:T(1,128)} %param.17) | copy-start | bytes 100
  43.1 143.3 %reduce-scatter.5.cloned.1.call-start = ((), (), s32[]{:S(2)}) async-start(), calls=%async_computation.3 | async-start | bytes 278528 | tf_op jit(solution)/shard_map/reduce_scatter | solution.py:145
  96.9 1.2 collective-permute-start
  101.8 4.0 %collective-permute-start.1 = (f32[8,4]{0,1:T(4,128)S(1)}, f32[8,4]{0,1:T(4,128)S(1)}, u32[]{:S(2)}, u32[]{:S(2)}) collective-permute-start(f32[8,4]{0,1:T(4,128)S(1)} %select_bitcast_fusion.2), channel_id=1, source_target_pairs={{0,1},{1,0},{2,3},{3,2},{4,5},{5,4},{6,7},{7,6},{8,9},{9,8},{10,11... | collective-permute-start | bytes 392 | tf_op jit(solution)/shard_map/ppermute | solution.py:19
  102.3 3.5 %collective-permute-start.3 = (f32[8,4]{0,1:T(4,128)S(1)}, f32[8,4]{0,1:T(4,128)S(1)}, u32[]{:S(2)}, u32[]{:S(2)}) collective-permute-start(f32[8,4]{0,1:T(4,128)S(1)} %select_bitcast_fusion.1), channel_id=1, source_target_pairs={{0,1},{1,0},{2,3},{3,2},{4,5},{5,4},{6,7},{7,6},{8,9},{9,8},{10,11... | collective-permute-start | bytes 392 | tf_op jit(solution)/shard_map/ppermute | solution.py:19
  105.6 1.2 collective-permute-start.2
  132.9 0.7 copy-start.1
Sparse Core Ops, SparseCore 0:
  43.3 52.8 reduce-scatter.2
  133.8 52.5 reduce-scatter.4
where the time goes:
time: 195 us
  waiting for transfers between devices  107 us (55%)
  blocking collectives  43.5 us (22%)
  matrix products  18.4 us (9%)
  between operations  13.7 us (7%)
  local copies, waits for them, and re-layouts  5.86 us (3%)
  other arithmetic  4.78 us (2%)
    reduce_scatter x1, waiting for transfers between devices, local(): lax.psum_scatter(proj_term, 'tp', scatter_dimension=0, tiled=True)  52.8 us
    reduce_scatter x1, waiting for transfers between devices, local(): my_cols = lax.psum_scatter(out_term, 'tp', scatter_dimension=0, tiled=True)  52.8 us
    all_gather x1, blocking collectives, local(): every_rows = lax.all_gather(hidden_in, 'tp', axis=0, tiled=True)  23.8 us
    all_gather x1, blocking collectives, local(): every_attn = lax.all_gather(attention[None], 'tp', axis=0, tiled=True)  19.8 us
    dot_general x1, matrix products, local(): jnp.einsum('gabe,cae->gbc', chosen, o_blocks[0], preferred_element_type=j...  5.65 us
    dot_general x1, matrix products, local(): jnp.einsum('rc,aec->rae', col_rows, q_blocks[0], preferred_element_type=j...  5.65 us
  transfers between devices with their start and end apart: 6, of which 4 were waited for; matrix products, arithmetic and copies ran while one was open for 2% of the time, Pallas kernels for 0%

commit v1 on v0

--- a/solution.py
+++ b/solution.py
@@ -19,6 +19,13 @@
     return lax.ppermute(value, axis, pairs)
 
 
+def pick(value, ids, axis):
+    slices = [
+        lax.dynamic_index_in_dim(value, ids[n], axis, keepdims=True) for n in range(ids.shape[0])
+    ]
+    return jnp.concatenate(slices, axis)
+
+
 def norm_rows(rows_float, norm_gain):
     mean_square = jnp.mean(rows_float * rows_float, axis=-1, keepdims=True)
     return (rows_float * lax.rsqrt(mean_square + 1e-05) * norm_gain[None, :]).astype(jnp.bfloat16)
@@ -37,11 +44,9 @@
     key_width = kv_blocks.shape[2]
     grid_row = my_index // grid_cols
     grid_col = my_index % grid_cols
-    dest_ids = jnp.arange(ranks, dtype=jnp.int32)
-    dest_rank = dest_ids % ROLL
-    dest_head = kv_assign[dest_rank]
+    dest_rank = jnp.arange(ROLL, dtype=jnp.int32)
+    dest_head = kv_assign
     dest_group = 2 * dest_head + dest_rank % 2
-    dest_copy = dest_ids // ROLL
     every_rows = lax.all_gather(hidden_in, "tp", axis=0, tiled=True)
     rows_float = (
         every_rows.reshape(group_count, ROLL, ROWS, DS)
@@ -57,9 +62,8 @@
     query_part = (
         query_part.reshape(group_count, ROWS, QG, HD)
         .transpose(0, 2, 1, 3)
-        .reshape(group_count * QG, ROWS, HD)
     )
-    query_pick = jnp.take(query_part, dest_copy * QG + dest_group, axis=0)
+    query_pick = pick(query_part, dest_group, 1).reshape(ranks, ROWS, HD)
     slot_mask = (jnp.arange(GR, dtype=jnp.int32) == grid_row).astype(jnp.float32)
     query_term = (query_pick[:, :, None, :] * slot_mask[None, None, :, None]).reshape(
         ranks, ROWS, GR * HD
@@ -69,9 +73,9 @@
     keyval_part = (
         keyval_part.reshape(group_count, ROWS, 2, KVH, HD)
         .transpose(0, 3, 1, 2, 4)
-        .reshape(group_count * KVH, ROWS, 2 * HD)
+        .reshape(group_count, KVH, ROWS, 2 * HD)
     )
-    keyval_term = jnp.take(keyval_part, dest_copy * KVH + dest_head, axis=0)
+    keyval_term = pick(keyval_part, dest_head, 1).reshape(ranks, ROWS, 2 * HD)
     proj_term = jnp.concatenate([query_term, keyval_term], -1).reshape(ranks * ROWS, (GR + 2) * HD)
     projected = lax.psum_scatter(proj_term, "tp", scatter_dimension=0, tiled=True)
     queries = projected[:, : GR * HD].astype(jnp.bfloat16)
@@ -135,7 +139,7 @@
     rank_of_slot = 2 * inverse[slot_ids // 2] + slot_ids % 2
     attn_grid = every_attn.reshape(group_count, ROLL, ROWS, GR, HD)
     row_slot = lax.dynamic_index_in_dim(attn_grid, grid_row, 3, keepdims=False)
-    chosen = jnp.take(row_slot, rank_of_slot, axis=1)
+    chosen = pick(row_slot, rank_of_slot, 1)
     out_part = jnp.einsum("gabe,cae->gbc", chosen, o_blocks[0], preferred_element_type=jnp.float32)
     placed = jnp.zeros((group_count, ROWS, D), jnp.float32)
     placed = lax.dynamic_update_slice_in_dim(placed, out_part, grid_col * col_width, 2)

time: 195 us -> 257 us (1.32)
  between operations: 13.7 us -> 104 us
  waiting for transfers between devices: 107 us -> 76.9 us
    reduce_scatter x1, waiting for transfers between devices: 52.8 us -> 22.2 us  [local(): lax.psum_scatter(proj_term, 'tp', scatter_dimension=0, tiled=True)]
    slice x0 -> x3, local copies, waits for them, and re-layouts: none -> 3.37 us  [pick(): ids[n]]
    gather x4 -> x0, local copies, waits for them, and re-layouts: 3.04 us -> none  [the longest x1 1.32 us: local(): dest_head = kv_assign[dest_rank]]
where the time goes in v1:
time: 257 us; the launch traced here: 255 us
  between operations  104 us (40%)
  waiting for transfers between devices  76.9 us (30%)
  blocking collectives  43.6 us (17%)
  matrix products  18.4 us (7%)
  local copies, waits for them, and re-layouts  6.51 us (3%)
  other arithmetic  5.22 us (2%)
    reduce_scatter x1, waiting for transfers between devices, local(): my_cols = lax.psum_scatter(out_term, 'tp', scatter_dimension=0, tiled=True)  52.7 us
    all_gather x1, blocking collectives, local(): every_rows = lax.all_gather(hidden_in, 'tp', axis=0, tiled=True)  23.8 us
    reduce_scatter x1, waiting for transfers between devices, local(): lax.psum_scatter(proj_term, 'tp', scatter_dimension=0, tiled=True)  22.2 us
    all_gather x1, blocking collectives, local(): every_attn = lax.all_gather(attention[None], 'tp', axis=0, tiled=True)  19.8 us
    dot_general x1, matrix products, local(): jnp.einsum('gabe,cae->gbc', chosen, o_blocks[0], preferred_element_type=j...  5.66 us
    dot_general x1, matrix products, local(): jnp.einsum('rc,aec->rae', col_rows, q_blocks[0], preferred_element_type=j...  5.65 us
  transfers between devices with their start and end apart: 6, of which 4 were waited for; matrix products, arithmetic and copies ran while one was open for 2% of the time, Pallas kernels for 0%

profile of v1, /device:TPU:0, one launch (start us, length us, event | category | flops | bytes accessed | tf_op | source)
XLA Modules:
  0.0 255.4 jit_solution(3000413255928679260)
XLA Ops:
  6.5 0.0 copy-start
  6.5 0.0 reduce-scatter.3.cloned.1.call-start
  6.5 23.8 %all_gather.6 = bf16[16,8,512]{2,1,0:T(8,128)(2,1)S(1)} all-gather(bf16[1,8,512]{2,1,0:T(8,128)(2,1)} %param.9), channel_id=1, replica_groups=mesh['groups'=2,'tp'=16] {'tp'}, dimensions={0}, use_global_device_ids=true | all-gather | bytes 139264 | tf_op jit(solution)/shard_map/all_gather | solution.py:50
  30.3 0.2 multiply_reduce_fusion
  30.5 0.7 slice.226
  31.3 0.1 select_reduce_fusion.1
  31.4 0.7 gather_fusion
  32.1 0.7 multiply_add_fusion
  32.7 0.7 fusion.84
  53.9 1.9 fusion.85
  75.6 0.1 broadcast_bitcast_fusion
  75.7 0.9 multiply_convert_fusion
  76.5 0.0 copy-done
  76.5 0.6 convolution_bitcast_fusion
  77.2 0.0 copy-start.2
  77.2 5.7 %fusion = f32[8,16,128]{2,0,1:T(8,128)S(1)} fusion(bf16[1,16,128,2048]{3,2,1,0:T(8,128)(2,1)} %param.11, bf16[8,8192]{1,0:T(8,128)(2,1)S(1)} %multiply_convert_fusion, s32[]{:T(128)S(6)} %select_n.322), kind=kOutput, calls=%fused_computation.1 | convolution fusion | flops 67108864 | bytes 8486916 | tf_op jit(solution)/shard_map/rc,aec->rae/dot_general | solution.py:59
  103.5 0.8 pad_maximum_fusion
  104.3 0.0 reduce-scatter.3.cloned.1.call-update
  104.3 0.0 reduce-scatter.5.cloned.1.call-start
  104.4 0.7 fusion.83
  135.0 0.0 copy-done.2
  135.0 0.1 iota_compare_fusion
  135.0 22.2 %reduce-scatter.3.cloned.1.call-done = f32[8,768]{1,0:T(8,128)} async-done(((f32[128,768]{1,0:T(8,128)}), f32[8,768]{1,0:T(8,128)}) %reduce-scatter.3.cloned.1.call-update) | async-done | bytes 24592 | tf_op jit(solution)/shard_map/reduce_scatter | solution.py:80
  157.3 0.7 convert.7
  158.0 0.0 collective-permute-start
  158.1 1.2 collective-permute-done
  159.2 0.1 fusion.53
  159.3 3.5 %select_reduce_fusion = (f32[8,8]{1,0:T(8,128)S(1)}, f32[8,8,2048]{2,1,0:T(8,128)S(1)}) fusion(pred[8,2048]{1,0:T(8,128)(4,1)S(1)} %iota_compare_fusion, bf16[1,8,2048,128]{3,2,1,0:T(8,128)(2,1)} %param.15, bf16[8,4,128]{2,1,0:T(4,128)(2,1)S(1)} %concatenate.32, bf16[8,4,128]{2,1,0:T(4,128)(2,1)S(1)} %concatenate.31, pred[]{:T(512)S(6)} %eq.35), kind=kOutput, calls=%fused_computation.15 | convolution fusion | flops 34021312 | bytes 4751617 | tf_op jit(solution)/shard_map/bhe,bte->bht/dot_general | solution.py:94
  162.8 0.1 copy.45
  162.9 0.2 collective-permute-start.1
  163.1 0.3 fusion.20
  163.3 0.1 copy.50
  163.4 0.3 collective-permute-start.3
  163.8 2.9 %fusion.17 = f32[8,8,128]{2,1,0:T(8,128)S(1)} fusion(bf16[1,8,2048,128]{3,2,1,0:T(8,128)(2,1)} %param.16, f32[8,8,2048]{2,1,0:T(8,128)S(1)} %get-tuple-element.61, f32[8,8]{1,0:T(8,128)S(1)} %fusion.55, pred[8,2048]{1,0:T(8,128)(4,1)S(1)} %iota_compare_fusion, f32[8,128]{1,0:T(8,128)S(1)} %get-tuple-element.8, f32[8,8]{1,0:T(8,128)S(1)} %convert_element_type.57), kind=kOutput, calls=%fused_computation.13 | convolution fusion | flops 33964032 | bytes 4772352 | tf_op jit(solution)/shard_map/bht,bte->bhe/dot_general | solution.py:107
  166.7 0.2 collective-permute-start.2
  166.9 0.0 collective-permute-done.1
  166.9 0.0 collective-permute-done.3
  167.0 0.1 copy.46
  167.0 0.1 copy.49
  167.1 0.1 copy.51
  167.2 0.8 collective-permute-done.2
  168.0 0.1 fusion.33
  168.1 19.8 %all_gather.7 = bf16[16,8,512]{2,1,0:T(8,128)(2,1)S(1)} all-gather(bf16[1,8,512]{2,1,0:T(8,128)(2,1)S(1)} %broadcast_in_dim_reshape.4), channel_id=1, replica_groups=mesh['groups'=2,'tp'=16] {'tp'}, dimensions={0}, use_global_device_ids=true | all-gather | bytes 139264 | tf_op jit(solution)/shard_map/all_gather | solution.py:132
  188.2 5.7 %fusion.14 = f32[1,8,8192]{2,1,0:T(8,128)S(1)} fusion(f32[1,8,8192]{2,1,0:T(8,128)S(1)} %broadcast_in_dim.42, s32[]{:T(128)S(6)} %select_n.322, bf16[2048,16,128]{2,1,0:T(8,128)(2,1)} %bitcast.288, bf16[1,16,8,128]{3,2,1,0:T(8,128)(2,1)S(1)} %constant_dynamic-update-slice_fusion.32), kind=kOutput, calls=%fused_computation.11 | convolution fusion | flops 67108864 | bytes 8486916 | tf_op jit(solution)/shard_map/gabe,cae->gbc/dot_general | solution.py:143
  193.8 0.7 copy-done.1
  194.5 0.0 reduce-scatter.5.cloned.1.call-update
  194.5 52.7 %reduce-scatter.5.cloned.1.call-done = f32[8,512]{1,0:T(8,128)} async-done(((f32[128,512]{1,0:T(8,128)}), f32[8,512]{1,0:T(8,128)}) %reduce-scatter.5.cloned.1.call-update) | async-done | bytes 16400 | tf_op jit(solution)/shard_map/reduce_scatter | solution.py:149
  247.3 1.3 convert_bitcast_fusion
  (69 shorter events, 0.7 us)
Async XLA Ops:
  6.5 70.0 %copy-start = (bf16[2,1024,512]{2,1,0:T(8,128)(2,1)S(1)}, bf16[2,1024,512]{2,1,0:T(8,128)(2,1)}, u32[]{:S(2)}) copy-start(bf16[2,1024,512]{2,1,0:T(8,128)(2,1)} %param.13) | copy-start | bytes 6291460
  6.5 150.7 %reduce-scatter.3.cloned.1.call-start = ((), (), s32[]{:S(2)}) async-start(), calls=%async_computation.2 | async-start | bytes 417792 | tf_op jit(solution)/shard_map/reduce_scatter | solution.py:80
  77.2 57.8 %copy-start.2 = (s32[1,8]{1,0:T(1,128)S(1)}, s32[1,8]{1,0:T(1,128)}, u32[]{:S(2)}) copy-start(s32[1,8]{1,0:T(1,128)} %param.17) | copy-start | bytes 100
  104.3 143.0 %reduce-scatter.5.cloned.1.call-start = ((), (), s32[]{:S(2)}) async-start(), calls=%async_computation.3 | async-start | bytes 278528 | tf_op jit(solution)/shard_map/reduce_scatter | solution.py:149
  158.0 1.2 collective-permute-start
  162.9 4.0 %collective-permute-start.1 = (f32[8,4]{0,1:T(4,128)S(1)}, f32[8,4]{0,1:T(4,128)S(1)}, u32[]{:S(2)}, u32[]{:S(2)}) collective-permute-start(f32[8,4]{0,1:T(4,128)S(1)} %select_bitcast_fusion.2), channel_id=1, source_target_pairs={{0,1},{1,0},{2,3},{3,2},{4,5},{5,4},{6,7},{7,6},{8,9},{9,8},{10,11... | collective-permute-start | bytes 392 | tf_op jit(solution)/shard_map/ppermute | solution.py:19
  163.4 3.5 %collective-permute-start.3 = (f32[8,4]{0,1:T(4,128)S(1)}, f32[8,4]{0,1:T(4,128)S(1)}, u32[]{:S(2)}, u32[]{:S(2)}) collective-permute-start(f32[8,4]{0,1:T(4,128)S(1)} %select_bitcast_fusion.1), channel_id=1, source_target_pairs={{0,1},{1,0},{2,3},{3,2},{4,5},{5,4},{6,7},{7,6},{8,9},{9,8},{10,11... | collective-permute-start | bytes 392 | tf_op jit(solution)/shard_map/ppermute | solution.py:19
  166.7 1.2 collective-permute-start.2
  193.8 0.7 copy-start.1
Sparse Core Ops, SparseCore 0:
  104.4 52.8 reduce-scatter.2
  194.7 52.5 reduce-scatter.4

commit v2 on v1

--- a/solution.py
+++ b/solution.py
@@ -1,6 +1,8 @@
 import jax
 import jax.numpy as jnp
 from jax import lax
+from jax.experimental import pallas as pl
+from jax.experimental.pallas import tpu as pltpu
 from jax.sharding import PartitionSpec as P
 
 D = 8192
@@ -150,9 +152,315 @@
     return my_cols.astype(jnp.bfloat16)[None]
 
 
+def pair_kernel(
+    hidden_ref, gain_ref, assign_ref, lengths_ref, q_hbm, o_hbm, kv_hbm, key_hbm, value_hbm,
+    out_ref,
+    q_ref, o_ref, ot_ref, kv_ref, key_ref, value_ref,
+    x_send, x_recv, sq_send, sq_recv, qpart, kvpart, q_send, q_recv, kv_send, kv_recv,
+    queries, stats, stats_recv, at_send, at_recv, normed, ordered, part_send, part_recv,
+    load_sem, qload_sem, x_ssem, x_rsem, sq_ssem, sq_rsem, q_ssem, q_rsem, kv_ssem, kv_rsem,
+    st_ssem, st_rsem, at_ssem, at_rsem, part_ssem, part_rsem,
+):
+    me = lax.axis_index("tp")
+    row = me // GR
+    col = me % GR
+    half = me % 2
+    bf16 = jnp.bfloat16
+    f32 = jnp.float32
+
+    def remote(src, dst, send, recv, dest):
+        return pltpu.make_async_remote_copy(
+            src_ref=src, dst_ref=dst, send_sem=send, recv_sem=recv,
+            device_id={"tp": dest}, device_id_type=pl.DeviceIdType.MESH,
+        )
+
+    def peers(body):
+        def step(p, carry):
+            body(lax.rem(me + p, ROLL))
+            return carry
+        lax.fori_loop(1, ROLL, step, 0)
+
+    barrier = pltpu.get_barrier_semaphore()
+    peers(lambda peer: pl.semaphore_signal(
+        barrier, inc=1, device_id={"tp": peer}, device_id_type=pl.DeviceIdType.MESH))
+
+    kv_load = pltpu.make_async_copy(kv_hbm, kv_ref, load_sem.at[0])
+    kv_load.start()
+    q_loads = []
+    for n in range(KVH):
+        span = pl.ds(n * 256, 256)
+        q_loads.append(pltpu.make_async_copy(q_hbm.at[span], q_ref.at[span], qload_sem.at[n]))
+        q_loads[n].start()
+
+    own = hidden_ref[0].astype(f32)
+    packed = jnp.concatenate([own[:, :256], own[:, 256:]], 0).astype(bf16)
+    x_send[...] = packed
+    squares = jnp.sum(own * own, axis=-1, keepdims=True)
+    diagonal = lax.broadcasted_iota(jnp.int32, (ROWS, 128), 0) == lax.broadcasted_iota(
+        jnp.int32, (ROWS, 128), 1)
+    sq_row = jnp.sum(jnp.where(diagonal, squares, 0.0), axis=0, keepdims=True)
+    sq_send[0] = sq_row
+    sq_recv[me] = sq_row
+
+    @pl.when(row == col)
+    def _():
+        x_recv[col] = packed
+
+    @pl.when(half == 1)
+    def _():
+        kv_recv[...] = jnp.zeros_like(kv_recv)
+
+    pl.semaphore_wait(barrier, ROLL - 1)
+    peers(lambda peer: remote(
+        sq_send.at[0], sq_recv.at[me], sq_ssem.at[peer], sq_rsem.at[me], peer).start())
+
+    def x_copy(i):
+        return remote(x_send, x_recv.at[col], x_ssem.at[i], x_rsem.at[col], GR * i + row)
+
+    for i in range(GR):
+        pl.when(GR * i + row != me)(lambda i=i: x_copy(i).start())
+
+    o_load = pltpu.make_async_copy(o_hbm, o_ref, load_sem.at[1])
+    key_load = pltpu.make_async_copy(key_hbm, key_ref, load_sem.at[2])
+    value_load = pltpu.make_async_copy(value_hbm, value_ref, load_sem.at[3])
+    o_load.start()
+    key_load.start()
+    value_load.start()
+
+    peers(lambda peer: remote(
+        sq_send.at[0], sq_recv.at[peer], sq_ssem.at[peer], sq_rsem.at[peer], peer).wait_recv())
+    total_sq = jnp.sum(sq_recv[...], axis=0)
+    mean_sq = jnp.sum(jnp.where(diagonal, total_sq, 0.0), axis=-1, keepdims=True) * (1.0 / D)
+    inv_root = lax.rsqrt(mean_sq + 1e-05)
+
+    own_normed = jnp.concatenate([
+        own[:, t * 128:(t + 1) * 128] * inv_root * gain_ref[pl.ds(me * 4 + t, 1), :]
+        for t in range(4)], 1).astype(bf16)
+    kv_load.wait()
+    contract = (((1,), (1,)), ((), ()))
+    for c in range(2):
+        made = lax.dot_general(own_normed, kv_ref[c], contract, preferred_element_type=f32)
+        for g in range(KVH):
+            kvpart[g, :, c * HD:(c + 1) * HD] = made[:, g * HD:(g + 1) * HD]
+
+    def kv_copy(m):
+        return remote(
+            kv_send.at[m], kv_recv.at[me], kv_ssem.at[m], kv_rsem.at[me], 2 * m)
+
+    def kv_step(m, carry):
+        term = kvpart[assign_ref[2 * m]]
+        kv_send[m] = term
+
+        @pl.when(2 * m == me)
+        def _():
+            kv_recv[me] = term
+
+        pl.when(2 * m != me)(lambda: kv_copy(m).start())
+        return carry
+    lax.fori_loop(0, KVH, kv_step, 0)
+
+    for k in range(GR):
+        pl.when(GR * col + k != me)(lambda k=k: remote(
+            x_send, x_recv.at[k], x_ssem.at[k], x_rsem.at[k], GR * col + k).wait_recv())
+        block = x_recv[k].astype(f32)
+        for t in range(4):
+            lo = (t % 2) * 128
+            tile = block[(t // 2) * ROWS:(t // 2 + 1) * ROWS, lo:lo + 128]
+            gain = gain_ref[pl.ds(16 * col + 4 * k + t, 1), :]
+            at = k * 512 + t * 128
+            normed[:, at:at + 128] = (tile * inv_root * gain).astype(bf16)
+    for n in range(KVH):
+        q_loads[n].wait()
+        qpart[n] = lax.dot_general(
+            normed[...], q_ref[n * 256:(n + 1) * 256, :], contract, preferred_element_type=f32)
+
+    q_own = qpart[assign_ref[me]]
+    q_recv[me] = q_own
+
+    def q_start(peer):
+        q_send[peer] = qpart[assign_ref[peer]]
+        remote(q_send.at[peer], q_recv.at[me], q_ssem.at[peer], q_rsem.at[me], peer).start()
+    peers(q_start)
+
+    o_load.wait()
+    r_ids = lax.broadcasted_iota(jnp.int32, (256, 256), 0)
+    c_ids = lax.broadcasted_iota(jnp.int32, (256, 256), 1)
+    shuffle = jnp.where(c_ids == (r_ids % 16) * 16 + r_ids // 16, 1.0, 0.0).astype(bf16)
+
+    def turn(n, carry):
+        base = pl.multiple_of(n * 512, 512)
+        rhs = jnp.concatenate(
+            [o_ref[pl.ds(base, 256), :], o_ref[pl.ds(base + 256, 256), :]], 1)
+        turned = jnp.dot(shuffle, rhs, preferred_element_type=f32).astype(bf16)
+        to = pl.multiple_of(n * 32, 32)
+        for a in range(QG):
+            for u in range(2):
+                ot_ref[pl.ds(to + 16 * u, 16), a * HD:(a + 1) * HD] = turned[
+                    a * 16:(a + 1) * 16, u * 128:(u + 1) * 128]
+        return carry
+    lax.fori_loop(0, 64, turn, 0)
+
+    @pl.when(half == 0)
+    def _():
+        peers(lambda peer: remote(
+            kv_send.at[0], kv_recv.at[peer], kv_ssem.at[0], kv_rsem.at[peer], peer).wait_recv())
+    peers(lambda peer: remote(
+        q_send.at[peer], q_recv.at[peer], q_ssem.at[peer], q_rsem.at[peer], peer).wait_recv())
+    for i in range(GR):
+        q_sum = (q_recv[4 * i] + q_recv[4 * i + 1]) + (q_recv[4 * i + 2] + q_recv[4 * i + 3])
+        for s in range(2):
+            queries[:, s * GR + i, :] = q_sum[:, s * HD:(s + 1) * HD]
+    kv_new = jnp.sum(kv_recv[...], axis=0).astype(bf16).astype(f32)
+    key_load.wait()
+    value_load.wait()
+    scale = 1.0 / HD**0.5
+    positions = lax.broadcasted_iota(jnp.int32, (8, key_ref.shape[1]), 1)
+    for b in range(ROWS):
+        q_b = queries[b].astype(bf16)
+        scores = lax.dot_general(q_b, key_ref[b], contract, preferred_element_type=f32) * scale
+        masked = positions < lengths_ref[0, b]
+        scores = jnp.where(masked, scores, -1e30)
+        new_score = jnp.sum(
+            q_b.astype(f32) * kv_new[b:b + 1, :HD], axis=-1, keepdims=True) * scale
+        new_score = jnp.where(half == 0, new_score, -1e30)
+        top = jnp.maximum(jnp.max(scores, axis=-1, keepdims=True), new_score)
+        weights = jnp.where(masked, jnp.exp(scores - top), 0.0)
+        new_weight = jnp.exp(new_score - top)
+        total = jnp.sum(weights, axis=-1, keepdims=True) + new_weight
+        summed = jnp.dot(weights.astype(bf16), value_ref[b], preferred_element_type=f32)
+        summed = summed + new_weight.astype(bf16).astype(f32) * kv_new[b:b + 1, HD:]
+        stats[b, 0] = summed
+        stats[b, 1] = jnp.broadcast_to(top, (8, HD))
+        stats[b, 2] = jnp.broadcast_to(total, (8, HD))
+
+    st_copy = remote(
+        stats.at[pl.ds(4 * (1 - half), 4)], stats_recv, st_ssem, st_rsem, me + 1 - 2 * half)
+    st_copy.start()
+    st_copy.wait_recv()
+    for b in range(4):
+        mine = stats[4 * half + b]
+        got = stats_recv[b]
+        joint = jnp.maximum(mine[1], got[1])
+        f_mine = jnp.exp(mine[1] - joint)
+        f_got = jnp.exp(got[1] - joint)
+        merged = (mine[0] * f_mine + got[0] * f_got) / (mine[2] * f_mine + got[2] * f_got)
+        for s in range(2):
+            at_send[:, s * 4 + b, :] = merged[s * 4:(s + 1) * 4]
+
+    at_recv[me] = at_send[row]
+    peers(lambda peer: remote(
+        at_send.at[peer // GR], at_recv.at[me], at_ssem.at[peer], at_rsem.at[me], peer).start())
+    peers(lambda peer: remote(
+        at_send.at[0], at_recv.at[peer], at_ssem.at[peer], at_rsem.at[peer], peer).wait_recv())
+
+    for g in range(KVH):
+        place = jnp.int32(0)
+        for m in range(1, KVH):
+            place = jnp.where(assign_ref[2 * m] == g, m, place)
+        first = at_recv[2 * place]
+        second = at_recv[2 * place + 1]
+        for s in range(2):
+            a = 2 * g + s
+            ordered[:, a * HD:(a + 1) * HD] = jnp.concatenate(
+                [first[s * 4:(s + 1) * 4], second[s * 4:(s + 1) * 4]], 0).astype(bf16)
+
+    def part_copy(k):
+        return remote(
+            part_send.at[k], part_recv.at[row], part_ssem.at[k], part_rsem.at[row], GR * col + k)
+
+    for k in range(GR):
+        part = lax.dot_general(
+            ordered[...], ot_ref[k * 512:(k + 1) * 512, :], contract, preferred_element_type=f32)
+        part_send[k] = part
+
+        @pl.when(GR * col + k == me)
+        def _(part=part):
+            part_recv[row] = part
+
+        pl.when(GR * col + k != me)(lambda k=k: part_copy(k).start())
+    for i in range(GR):
+        pl.when(GR * i + row != me)(lambda i=i: remote(
+            part_send.at[0], part_recv.at[i], part_ssem.at[0], part_rsem.at[i],
+            GR * i + row).wait_recv())
+    out_ref[0] = (
+        (part_recv[0] + part_recv[1]) + (part_recv[2] + part_recv[3])).astype(bf16)
+
+    def drain(peer):
+        remote(sq_send.at[0], sq_recv.at[me], sq_ssem.at[peer], sq_rsem.at[me], peer).wait_send()
+        remote(q_send.at[peer], q_recv.at[me], q_ssem.at[peer], q_rsem.at[me], peer).wait_send()
+        remote(at_send.at[0], at_recv.at[me], at_ssem.at[peer], at_rsem.at[me], peer).wait_send()
+    peers(drain)
+    for m in range(KVH):
+        pl.when(2 * m != me)(lambda m=m: kv_copy(m).wait_send())
+    for i in range(GR):
+        pl.when(GR * i + row != me)(lambda i=i: x_copy(i).wait_send())
+        pl.when(GR * col + i != me)(lambda i=i: part_copy(i).wait_send())
+    st_copy.wait_send()
+
+
+def one_group(
+    hidden_in, norm_gain, q_blocks, o_blocks, kv_blocks, kv_assign, key_cache, value_cache, lengths
+):
+    f32, bf16 = jnp.float32, jnp.bfloat16
+    ctx = key_cache.shape[2]
+    vmem = pl.BlockSpec(memory_space=pltpu.VMEM)
+    smem = pl.BlockSpec(memory_space=pltpu.SMEM)
+    hbm = pl.BlockSpec(memory_space=pl.ANY)
+    dma = pltpu.SemaphoreType.DMA
+    return pl.pallas_call(
+        pair_kernel,
+        out_shape=jax.ShapeDtypeStruct((1, ROWS, DS), bf16),
+        in_specs=[vmem, vmem, smem, smem, hbm, hbm, hbm, hbm, hbm],
+        out_specs=vmem,
+        scratch_shapes=[
+            pltpu.VMEM((2048, 2048), bf16),
+            pltpu.VMEM((32768, 128), bf16),
+            pltpu.VMEM((2048, 2048), bf16),
+            pltpu.VMEM((2, 1024, DS), bf16),
+            pltpu.VMEM((ROWS, ctx, HD), bf16),
+            pltpu.VMEM((ROWS, ctx, HD), bf16),
+            pltpu.VMEM((16, 256), bf16),
+            pltpu.VMEM((GR, 16, 256), bf16),
+            pltpu.VMEM((1, 1, 128), f32),
+            pltpu.VMEM((ROLL, 1, 128), f32),
+            pltpu.VMEM((KVH, ROWS, 256), f32),
+            pltpu.VMEM((KVH, ROWS, 256), f32),
+            pltpu.VMEM((ROLL, ROWS, 256), f32),
+            pltpu.VMEM((ROLL, ROWS, 256), f32),
+            pltpu.VMEM((KVH, ROWS, 256), f32),
+            pltpu.VMEM((ROLL, ROWS, 256), f32),
+            pltpu.VMEM((ROWS, 8, HD), f32),
+            pltpu.VMEM((ROWS, 3, 8, HD), f32),
+            pltpu.VMEM((4, 3, 8, HD), f32),
+            pltpu.VMEM((GR, 8, HD), f32),
+            pltpu.VMEM((ROLL, 8, HD), f32),
+            pltpu.VMEM((ROWS, 2048), bf16),
+            pltpu.VMEM((ROWS, 2048), bf16),
+            pltpu.VMEM((GR, ROWS, DS), f32),
+            pltpu.VMEM((GR, ROWS, DS), f32),
+            dma((4,)), dma((KVH,)),
+            dma((GR,)), dma((GR,)),
+            dma((ROLL,)), dma((ROLL,)),
+            dma((ROLL,)), dma((ROLL,)),
+            dma((KVH,)), dma((ROLL,)),
+            dma, dma,
+            dma((ROLL,)), dma((ROLL,)),
+            dma((GR,)), dma((GR,)),
+        ],
+        compiler_params=pltpu.CompilerParams(
+            collective_id=0, has_side_effects=True, vmem_limit_bytes=56 * 2**20),
+        cost_estimate=pl.CostEstimate(
+            flops=2 * 8 * 11 * 2**20, bytes_accessed=26 * 2**20, transcendentals=8 * 8 * ctx),
+    )(
+        hidden_in, norm_gain.reshape(-1, 128), kv_assign, lengths,
+        q_blocks.reshape(2048, 2048), o_blocks.reshape(-1, HD), kv_blocks,
+        key_cache[0], value_cache[0],
+    )
+
+
 def solution(mesh):
     return jax.shard_map(
-        local,
+        one_group if mesh.shape["tp"] == ROLL else local,
         mesh=mesh,
         in_specs=(
             P(("groups", "tp"), None, None),

time: 257 us -> 46.3 us (0.18)
  between operations: 104 us -> 0.01 us
  waiting for transfers between devices: 76.9 us -> 0 us
  Pallas kernels: 0 us -> 44.4 us
  blocking collectives: 43.6 us -> 0 us
  matrix products: 18.4 us -> 0 us
  other arithmetic: 5.22 us -> 0 us
  local copies, waits for them, and re-layouts: 6.51 us -> 1.3 us
    reduce_scatter x2 -> x0, waiting for transfers between devices: 75 us -> none  [the longest x1 52.7 us: local(): my_cols = lax.psum_scatter(out_term, 'tp', scatter_dimension=0, tiled=True)]
    pallas_call x0 -> x1, Pallas kernels: none -> 44.4 us  [one_group(): pl.pallas_call(pair_kernel, out_shape=jax.ShapeDtypeStruct((1, ROWS, DS),...]
    all_gather x2 -> x0, blocking collectives: 43.6 us -> none  [the longest x1 23.8 us: local(): every_rows = lax.all_gather(hidden_in, 'tp', axis=0, tiled=True)]
    dot_general x6 -> x0, matrix products: 18.4 us -> none  [the longest x1 5.66 us: local(): jnp.einsum('gabe,cae->gbc', chosen, o_blocks[0], preferred_element_type=j...]
    slice x5 -> x0, local copies, waits for them, and re-layouts: 4.12 us -> none  [the longest x3 3.37 us: pick(): ids[n]]
  transfers between devices with their start and end apart: 6 -> 0, of which waited for: 4 -> 0; matrix products, arithmetic and copies ran while one was open for 2% -> 0% of each run, Pallas kernels for 0% -> 0%
where the time goes in v2:
time: 46.3 us; the launch traced here: 45.7 us
  Pallas kernels  44.4 us (96%)
  local copies, waits for them, and re-layouts  1.3 us (3%)
    pallas_call x1, Pallas kernels, one_group(): pl.pallas_call(pair_kernel, out_shape=jax.ShapeDtypeStruct((1, ROWS, DS),...  44.4 us
    unnamed x1, local copies, waits for them, and re-layouts  1.3 us

profile of v2, /device:TPU:0, one launch (start us, length us, event | category | flops | bytes accessed | tf_op | source)
XLA Modules:
  0.0 45.7 jit_solution(3268017754232235815)
XLA Ops:
  0.0 44.4 %shard_map.91 = bf16[1,8,512]{2,1,0:T(8,128)(2,1)} custom-call(bf16[1,8,512]{2,1,0:T(8,128)(2,1)} %hidden_ref.1, f32[64,128]{1,0:T(8,128)} %bitcast.9, s32[16]{0:T(128)} %assign_ref.1, s32[1,8]{1,0:T(1,128)} %lengths_ref.1, bf16[2048,2048]{1,0:T(8,128)(2,1)} %bitcast.5, bf16[32768,128]{1,0:T(8,128)(2,1)} %bitcast.6, bf16[2,1024,512]{2,1,0:T(8,128)(2,1)} %kv_hbm.1, ...), custom_call_target="tpu_custom_call" | custom-call | flops 184549376 | bytes 27262976 | tf_op jit(solution)/shard_map/pallas_call | solution.py:410
  44.4 1.3 %copy.11 = bf16[1,8,512]{2,1,0:T(8,128)(2,1)} copy(bf16[1,8,512]{2,1,0:T(8,128)(2,1)} %shard_map.91) | data formatting | bytes 16384

commit v3 on v2

--- a/solution.py
+++ b/solution.py
@@ -298,7 +298,12 @@
                 ot_ref[pl.ds(to + 16 * u, 16), a * HD:(a + 1) * HD] = turned[
                     a * 16:(a + 1) * 16, u * 128:(u + 1) * 128]
         return carry
-    lax.fori_loop(0, 64, turn, 0)
+
+    def turn_four(n, carry):
+        for u in range(4):
+            turn(4 * n + u, carry)
+        return carry
+    lax.fori_loop(0, 16, turn_four, 0)
 
     @pl.when(half == 0)
     def _():

time: 46.3 us -> 38.6 us (0.83)
  Pallas kernels: 44.4 us -> 36.7 us
    pallas_call x1, Pallas kernels: 44.4 us -> 36.7 us  [one_group(): pl.pallas_call(pair_kernel, out_shape=jax.ShapeDtypeStruct((1, ROWS, DS),...]
where the time goes in v3:
time: 38.6 us; the launch traced here: 38 us
  Pallas kernels  36.7 us (95%)
  local copies, waits for them, and re-layouts  1.3 us (3%)
    pallas_call x1, Pallas kernels, one_group(): pl.pallas_call(pair_kernel, out_shape=jax.ShapeDtypeStruct((1, ROWS, DS),...  36.7 us
    unnamed x1, local copies, waits for them, and re-layouts  1.3 us

profile of v3, /device:TPU:0, one launch (start us, length us, event | category | flops | bytes accessed | tf_op | source)
XLA Modules:
  0.0 38.0 jit_solution(18057573062910582653)
XLA Ops:
  0.0 36.7 %shard_map.91 = bf16[1,8,512]{2,1,0:T(8,128)(2,1)} custom-call(bf16[1,8,512]{2,1,0:T(8,128)(2,1)} %hidden_ref.1, f32[64,128]{1,0:T(8,128)} %bitcast.9, s32[16]{0:T(128)} %assign_ref.1, s32[1,8]{1,0:T(1,128)} %lengths_ref.1, bf16[2048,2048]{1,0:T(8,128)(2,1)} %bitcast.5, bf16[32768,128]{1,0:T(8,128)(2,1)} %bitcast.6, bf16[2,1024,512]{2,1,0:T(8,128)(2,1)} %kv_hbm.1, ...), custom_call_target="tpu_custom_call" | custom-call | flops 184549376 | bytes 27262976 | tf_op jit(solution)/shard_map/pallas_call | solution.py:415
  36.7 1.3 %copy.11 = bf16[1,8,512]{2,1,0:T(8,128)(2,1)} copy(bf16[1,8,512]{2,1,0:T(8,128)(2,1)} %shard_map.91) | data formatting | bytes 16384

commit v4 on v3

--- a/solution.py
+++ b/solution.py
@@ -176,9 +176,10 @@
 
     def peers(body):
         def step(p, carry):
-            body(lax.rem(me + p, ROLL))
+            for u in range(1, 6):
+                body(lax.rem(me + 5 * p + u, ROLL))
             return carry
-        lax.fori_loop(1, ROLL, step, 0)
+        lax.fori_loop(0, (ROLL - 1) // 5, step, 0)
 
     barrier = pltpu.get_barrier_semaphore()
     peers(lambda peer: pl.semaphore_signal(

time: 38.6 us -> 38.4 us (level)
  no operation moved by 1% of the time
where the time goes in v4:
time: 38.4 us; the launch traced here: 37.9 us
  Pallas kernels  36.6 us (95%)
  local copies, waits for them, and re-layouts  1.3 us (3%)
    pallas_call x1, Pallas kernels, one_group(): pl.pallas_call(pair_kernel, out_shape=jax.ShapeDtypeStruct((1, ROWS, DS),...  36.6 us
    unnamed x1, local copies, waits for them, and re-layouts  1.3 us

profile of v4, /device:TPU:0, one launch (start us, length us, event | category | flops | bytes accessed | tf_op | source)
XLA Modules:
  0.0 37.9 jit_solution(7839482341043777115)
XLA Ops:
  0.0 36.6 %shard_map.91 = bf16[1,8,512]{2,1,0:T(8,128)(2,1)} custom-call(bf16[1,8,512]{2,1,0:T(8,128)(2,1)} %hidden_ref.1, f32[64,128]{1,0:T(8,128)} %bitcast.9, s32[16]{0:T(128)} %assign_ref.1, s32[1,8]{1,0:T(1,128)} %lengths_ref.1, bf16[2048,2048]{1,0:T(8,128)(2,1)} %bitcast.5, bf16[32768,128]{1,0:T(8,128)(2,1)} %bitcast.6, bf16[2,1024,512]{2,1,0:T(8,128)(2,1)} %kv_hbm.1, ...), custom_call_target="tpu_custom_call" | custom-call | flops 184549376 | bytes 27262976 | tf_op jit(solution)/shard_map/pallas_call | solution.py:416
  36.6 1.3 %copy.11 = bf16[1,8,512]{2,1,0:T(8,128)(2,1)} copy(bf16[1,8,512]{2,1,0:T(8,128)(2,1)} %shard_map.91) | data formatting | bytes 16384
